TPU v7x, 32 devices: a whole 2x2x4 slice. The times are simulated.
32 devices in a mesh: row: 8 (over z, x), col: 4 (over y, core).
Axes of the slice: x: 2, y: 2, z: 4, core: 2. Of those that a mesh axis runs over, the one named last changes fastest.
Arguments:
- records: bfloat16 [128, 8, 1500], P('row', 'col'), may hold values from -6 to 6
- channel_live: int32 [128], replicated, may hold values 0 or 1
- minute_valid: int32 [8], replicated, may hold values 0 or 1
Outputs:
- correlations: bfloat16 [128, 128, 801], P('row', 'col')
All inputs are finite; a program needn't handle non-finite values.
Results may differ from a plain program's by a relative error of at most 0.0075.
Values may be sent and summed in bfloat16 or wider, within the bound.
A program may use at most 64 MiB of HBM per device.

v0:
```python
import math
import jax
import jax.numpy as jnp
from jax import lax
from jax.sharding import PartitionSpec as P

F = 640
BAND = 32
MAXLAG = 400


def forward_table(length, nfreq):
    times = jnp.arange(length, dtype=jnp.int32)[:, None]
    freqs = jnp.arange(1, nfreq + 1, dtype=jnp.int32)[None, :]
    phase = (times * freqs % length).astype(jnp.float32) * jnp.float32(2.0 * math.pi / length)
    return jnp.concatenate([jnp.cos(phase), -jnp.sin(phase)], axis=1).astype(jnp.bfloat16)


def inverse_table(length, nfreq, maxlag):
    freqs = jnp.arange(1, nfreq + 1, dtype=jnp.int32)[:, None]
    shifts = jnp.arange(-maxlag, maxlag + 1, dtype=jnp.int32)[None, :]
    phase = jnp.mod(freqs * shifts, length).astype(jnp.float32) * jnp.float32(
        2.0 * math.pi / length
    )
    return jnp.concatenate([jnp.cos(phase), -jnp.sin(phase)], axis=0).astype(jnp.bfloat16)


def whiten(signal, live, valid, table, band):
    chans, mins, length = signal.shape
    nfreq = table.shape[1] // 2
    spectrum = jnp.dot(
        signal.reshape(chans * mins, length), table, preferred_element_type=jnp.float32
    )
    grouped = spectrum.reshape(chans, mins, 2, nfreq // band, band)
    power = jnp.mean(grouped * grouped, axis=(2, 4))
    weight = (
        lax.rsqrt(power + 1e-06)
        * live.astype(jnp.float32)[:, None, None]
        * valid.astype(jnp.float32)[None, :, None]
    )
    return (
        (grouped * weight[:, :, None, :, None]).reshape(chans, mins, 2 * nfreq).astype(jnp.bfloat16)
    )


def correlate(rows, cols, itab, count):
    nfreq = rows.shape[2] // 2
    row_real = rows[:, :, :nfreq]
    row_imag = rows[:, :, nfreq:]
    col_real = cols[:, :, :nfreq]
    col_imag = cols[:, :, nfreq:]
    real_sum = jnp.einsum(
        "imf,jmf->ijf", row_real, col_real, preferred_element_type=jnp.float32
    ) + jnp.einsum("imf,jmf->ijf", row_imag, col_imag, preferred_element_type=jnp.float32)
    imag_sum = jnp.einsum(
        "imf,jmf->ijf", row_imag, col_real, preferred_element_type=jnp.float32
    ) - jnp.einsum("imf,jmf->ijf", row_real, col_imag, preferred_element_type=jnp.float32)
    stacked = (jnp.concatenate([real_sum, imag_sum], axis=-1) / jnp.float32(count)).astype(
        jnp.bfloat16
    )
    lagged = jnp.dot(stacked.reshape(-1, 2 * nfreq), itab, preferred_element_type=jnp.float32)
    lagged = lagged * jnp.float32(1.0 / math.sqrt(nfreq))
    return lagged.astype(jnp.bfloat16).reshape(rows.shape[0], cols.shape[0], itab.shape[1])


def body(records, channel_live, minute_valid):
    row_total = lax.axis_size("row")
    col_total = lax.axis_size("col")
    row_count = records.shape[0]
    per_device = records.shape[1]
    length = records.shape[2]
    channels = row_count * row_total
    col_count = channels // col_total
    minutes = per_device * col_total
    col_index = lax.axis_index("col")
    row_start = lax.axis_index("row") * row_count
    row_live = lax.dynamic_slice_in_dim(channel_live, row_start, row_count)
    table = forward_table(length, F)
    own_valid = lax.dynamic_slice_in_dim(minute_valid, col_index * per_device, per_device)
    local = whiten(records, row_live, own_valid, table, BAND)
    row_spectra = lax.all_gather(local, "col", axis=1, tiled=True)
    every_channel = lax.all_gather(local, "row", axis=0, tiled=True)
    col_spectra = lax.all_to_all(every_channel, "col", split_axis=0, concat_axis=1, tiled=True)
    itab = inverse_table(length, F, MAXLAG)
    block = math.gcd(row_count, 8)
    grouped = row_spectra.reshape(row_count // block, block, minutes, 2 * F)

    def one_block(rows):
        return correlate(rows, col_spectra, itab, minutes)

    result = lax.map(one_block, grouped)
    return result.reshape(row_count, col_count, 2 * MAXLAG + 1)


def solution(mesh):
    in_specs = (P("row", "col", None), P(), P())
    out_specs = P("row", "col", None)
    return jax.shard_map(body, mesh=mesh, in_specs=in_specs, out_specs=out_specs, check_vma=False)
```

profile of v0, /device:TPU:0, one launch (start us, length us, event | category | flops | bytes accessed | tf_op | source)
XLA Modules:
  0.0 129.4 jit_solution(9751996412103795063)
XLA Ops:
  0.0 17.2 %cosine_convert_fusion = (bf16[1500,640]{1,0:T(8,128)(2,1)S(1)}, bf16[1500,640]{1,0:T(8,128)(2,1)}) fusion(s32[640]{0:T(1024)S(1)} %iota_add_fusion.1), kind=kLoop, calls=%fused_computation.31 | loop fusion | flops 11520000 | bytes 3842560 | tf_op jit(solution)/shard_map/convert.2
  17.3 2.3 %fusion.45 = (f32[32,1280]{1,0:T(8,128)S(1)}, f32[32,1280]{1,0:T(8,128)S(1)}) fusion(bf16[32,1500]{1,0:T(8,128)(2,1)S(1)} %reshape.42, bf16[1500,640]{1,0:T(8,128)(2,1)} %get-tuple-element.61, bf16[1500,640]{1,0:T(8,128)(2,1)S(1)} %get-tuple-element.60), kind=kOutput, calls=%fused_computation.59 | convolution fusion | flops 130600960 | bytes 4263680 | tf_op jit(solution)/shard_map/dot_general | solution.py:31
  20.9 33.5 %all_gather.7 = bf16[128,2,1280]{2,0,1:T(8,128)(2,1)S(1)} all-gather(bf16[16,2,1280]{2,0,1:T(8,128)(2,1)S(1)} %fusion.39), channel_id=1, replica_groups=mesh['row'=8,'col'=4] {'row'}, dimensions={0}, use_global_device_ids=true | all-gather | bytes 737280 | tf_op jit(solution)/shard_map/all_gather | solution.py:82
  54.4 1.5 %copy.28 = bf16[128,2,1280]{2,1,0:T(2,128)(2,1)} copy(bf16[128,2,1280]{2,0,1:T(8,128)(2,1)S(1)} %all_gather.7) | data formatting | bytes 1310720 | tf_op jit(solution)/shard_map/all_gather | solution.py:82
  55.9 3.5 %all-to-all-start = ((bf16[128,2,1280]{2,1,0:T(2,128)(2,1)}), bf16[128,2,1280]{2,1,0:T(2,128)(2,1)S(1)}, u32[]{:S(2)}, u32[]{:S(2)}) async-start(bf16[128,2,1280]{2,1,0:T(2,128)(2,1)} %copy.28), calls=%async_computation | async-start | bytes 1310720 | tf_op jit(solution)/shard_map/all_to_all | solution.py:83
  59.4 10.2 %cosine_convert_fusion.1 = (bf16[640,801]{1,0:T(8,128)(2,1)S(1)}, bf16[640,801]{1,0:T(8,128)(2,1)S(1)}) fusion(s32[801]{0:T(1024)S(1)} %iota_add_fusion, s32[640]{0:T(1024)S(1)} %iota_add_fusion.1), kind=kLoop, calls=%fused_computation.41 | loop fusion | flops 6151680 | bytes 2056324 | tf_op jit(solution)/shard_map/convert
  69.6 6.8 %all_gather.6 = bf16[16,8,1280]{2,0,1:T(8,128)(2,1)S(1)} all-gather(bf16[16,2,1280]{2,0,1:T(8,128)(2,1)S(1)} %fusion.39), channel_id=1, replica_groups=mesh['row'=8,'col'=4] {'col'}, dimensions={1}, use_global_device_ids=true | all-gather | bytes 409600 | tf_op jit(solution)/shard_map/all_gather | solution.py:81
  76.4 1.6 %pad_maximum_fusion = bf16[1280,801]{1,0:T(8,128)(2,1)} fusion(bf16[640,801]{1,0:T(8,128)(2,1)S(1)} %get-tuple-element.59, bf16[640,801]{1,0:T(8,128)(2,1)S(1)} %get-tuple-element.58), kind=kLoop, calls=%fused_computation.39 | loop fusion | flops 4101120 | bytes 4101120 | tf_op jit(solution)/shard_map/concatenate | solution.py:25
  78.0 4.9 %copy.29 = bf16[32,4,2,1280]{0,2,1,3:T(2,128)(2,1)} copy(bf16[32,4,2,1280]{3,2,0,1:T(2,128)(2,1)S(1)} %bitcast.75) | data formatting | bytes 1310720 | tf_op jit(solution)/shard_map/all_to_all | solution.py:83
  82.9 46.5 %while.10 = (s32[]{:T(128)}, bf16[2,8,32,801]{3,2,1,0:T(8,128)(2,1)}, bf16[2,8,8,1280]{3,1,0,2:T(8,128)(2,1)S(1)}, bf16[32,8,1280]{0,1,2:T(8,128)(2,1)}, bf16[1280,801]{1,0:T(8,128)(2,1)}, /*index=5*/s32[]{:T(128)}) while((s32[]{:T(128)}, bf16[2,8,32,801]{3,2,1,0:T(8,128)(2,1)}, bf16[2,8,8,1280]{3,1,0,2:T(8,128)(2,1)S(1)}, ...), condition=%wide.region_2.3_spmd, body=%wide.region_1.2_spmd.sunk | while | flops 537149952 | bytes 34353424 | solution.py:91
  83.7 1.8 %copy.50 = bf16[1,8,8,1280]{2,1,3,0:T(8,128)(2,1)S(1)} copy(bf16[1,8,8,1280]{3,1,0,2:T(8,128)(2,1)S(1)} %constant_dynamic-slice_fusion.2) | data formatting | bytes 327680 | tf_op jit(solution)/shard_map/while/body/jit(dynamic_index_in_dim)/dynamic_slice | solution.py:91
  85.4 1.4 %fusion.98 = bf16[32,8,640]{0,1,2:T(8,128)(2,1)S(1)} fusion(bf16[32,8,1280]{0,1,2:T(8,128)(2,1)} %get-tuple-element.110), kind=kLoop, calls=%fused_computation.15.clone.1.clone.1 | loop fusion | bytes 655360 | tf_op jit(solution)/shard_map/while/body/eval_jaxpr/imf,jmf->ijf/dot_general | solution.py:54
  87.7 0.9 copy-done
  88.7 2.4 %add_bitcast_fusion.2 = f32[8,32,640]{1,0,2:T(8,128)} fusion(f32[640,8,32]{2,1,0:T(8,128)S(1)} %fusion.99, bf16[1,8,8,1280]{2,1,3,0:T(8,128)(2,1)S(1)} %copy.50, bf16[32,8,640]{0,1,2:T(8,128)(2,1)S(1)} %fusion.100), kind=kOutput, calls=%fused_computation.9.clone.2 | convolution fusion | flops 2785280 | bytes 1802240 | tf_op jit(solution)/shard_map/while/body/eval_jaxpr/imf,jmf->ijf/dot_general | solution.py:52
  91.0 3.0 %copy.52 = f32[8,32,640]{2,1,0:T(8,128)} copy(f32[8,32,640]{1,0,2:T(8,128)} %add_bitcast_fusion.2) | data formatting | bytes 1310720 | tf_op jit(solution)/shard_map/while/body/eval_jaxpr/add | solution.py:52
  94.1 1.4 %fusion.95 = bf16[32,8,640]{0,1,2:T(8,128)(2,1)S(1)} fusion(bf16[32,8,1280]{0,1,2:T(8,128)(2,1)} %get-tuple-element.110), kind=kLoop, calls=%fused_computation.16.clone.1.clone.1 | loop fusion | bytes 655360 | tf_op jit(solution)/shard_map/while/body/eval_jaxpr/imf,jmf->ijf/dot_general | solution.py:55
  96.3 0.9 copy-done.1
  97.3 2.4 %subtract_bitcast_fusion.2 = f32[8,32,640]{1,0,2:T(8,128)} fusion(f32[640,8,32]{2,1,0:T(8,128)S(1)} %fusion.96, bf16[1,8,8,1280]{2,1,3,0:T(8,128)(2,1)S(1)} %copy.50, bf16[32,8,640]{0,1,2:T(8,128)(2,1)S(1)} %fusion.97), kind=kOutput, calls=%fused_computation.8.clone.2 | convolution fusion | flops 2785280 | bytes 1802240 | tf_op jit(solution)/shard_map/while/body/eval_jaxpr/imf,jmf->ijf/dot_general | solution.py:57
  99.7 2.5 %copy.51 = f32[8,32,640]{2,1,0:T(8,128)S(1)} copy(f32[8,32,640]{1,0,2:T(8,128)} %subtract_bitcast_fusion.2) | data formatting | bytes 1310720 | tf_op jit(solution)/shard_map/while/body/eval_jaxpr/sub | solution.py:55
  102.2 2.7 %fusion.101 = bf16[256,801]{0,1:T(8,128)(2,1)S(1)} fusion(bf16[1280,801]{1,0:T(8,128)(2,1)} %get-tuple-element.111, f32[256,640]{1,0:T(8,128)S(1)} %bitcast.73, f32[256,640]{1,0:T(8,128)S(1)} %bitcast.72), kind=kOutput, calls=%fused_computation.13.clone.1 | convolution fusion | flops 526336512 | bytes 3771392 | tf_op jit(solution)/shard_map/while/body/eval_jaxpr/dot_general | solution.py:61
  105.2 0.9 copy-done.7
  106.9 1.8 %copy.50 = bf16[1,8,8,1280]{2,1,3,0:T(8,128)(2,1)S(1)} copy(bf16[1,8,8,1280]{3,1,0,2:T(8,128)(2,1)S(1)} %constant_dynamic-slice_fusion.2) | data formatting | bytes 327680 | tf_op jit(solution)/shard_map/while/body/jit(dynamic_index_in_dim)/dynamic_slice | solution.py:91
  108.7 1.4 %fusion.98 = bf16[32,8,640]{0,1,2:T(8,128)(2,1)S(1)} fusion(bf16[32,8,1280]{0,1,2:T(8,128)(2,1)} %get-tuple-element.110), kind=kLoop, calls=%fused_computation.15.clone.1.clone.1 | loop fusion | bytes 655360 | tf_op jit(solution)/shard_map/while/body/eval_jaxpr/imf,jmf->ijf/dot_general | solution.py:54
  110.9 0.9 copy-done
  111.9 2.4 %add_bitcast_fusion.2 = f32[8,32,640]{1,0,2:T(8,128)} fusion(f32[640,8,32]{2,1,0:T(8,128)S(1)} %fusion.99, bf16[1,8,8,1280]{2,1,3,0:T(8,128)(2,1)S(1)} %copy.50, bf16[32,8,640]{0,1,2:T(8,128)(2,1)S(1)} %fusion.100), kind=kOutput, calls=%fused_computation.9.clone.2 | convolution fusion | flops 2785280 | bytes 1802240 | tf_op jit(solution)/shard_map/while/body/eval_jaxpr/imf,jmf->ijf/dot_general | solution.py:52
  114.3 3.0 %copy.52 = f32[8,32,640]{2,1,0:T(8,128)} copy(f32[8,32,640]{1,0,2:T(8,128)} %add_bitcast_fusion.2) | data formatting | bytes 1310720 | tf_op jit(solution)/shard_map/while/body/eval_jaxpr/add | solution.py:52
  117.3 1.4 %fusion.95 = bf16[32,8,640]{0,1,2:T(8,128)(2,1)S(1)} fusion(bf16[32,8,1280]{0,1,2:T(8,128)(2,1)} %get-tuple-element.110), kind=kLoop, calls=%fused_computation.16.clone.1.clone.1 | loop fusion | bytes 655360 | tf_op jit(solution)/shard_map/while/body/eval_jaxpr/imf,jmf->ijf/dot_general | solution.py:55
  119.6 0.9 copy-done.1
  120.6 2.4 %subtract_bitcast_fusion.2 = f32[8,32,640]{1,0,2:T(8,128)} fusion(f32[640,8,32]{2,1,0:T(8,128)S(1)} %fusion.96, bf16[1,8,8,1280]{2,1,3,0:T(8,128)(2,1)S(1)} %copy.50, bf16[32,8,640]{0,1,2:T(8,128)(2,1)S(1)} %fusion.97), kind=kOutput, calls=%fused_computation.8.clone.2 | convolution fusion | flops 2785280 | bytes 1802240 | tf_op jit(solution)/shard_map/while/body/eval_jaxpr/imf,jmf->ijf/dot_general | solution.py:57
  122.9 2.5 %copy.51 = f32[8,32,640]{2,1,0:T(8,128)S(1)} copy(f32[8,32,640]{1,0,2:T(8,128)} %subtract_bitcast_fusion.2) | data formatting | bytes 1310720 | tf_op jit(solution)/shard_map/while/body/eval_jaxpr/sub | solution.py:55
  125.5 2.7 %fusion.101 = bf16[256,801]{0,1:T(8,128)(2,1)S(1)} fusion(bf16[1280,801]{1,0:T(8,128)(2,1)} %get-tuple-element.111, f32[256,640]{1,0:T(8,128)S(1)} %bitcast.73, f32[256,640]{1,0:T(8,128)S(1)} %bitcast.72), kind=kOutput, calls=%fused_computation.13.clone.1 | convolution fusion | flops 526336512 | bytes 3771392 | tf_op jit(solution)/shard_map/while/body/eval_jaxpr/dot_general | solution.py:61
  128.5 0.9 copy-done.7
  (56 shorter events, 7.1 us)
Async XLA Ops:
  0.0 17.2 %copy-start.5 = (bf16[16,2,1500]{2,1,0:T(2,128)(2,1)S(1)}, bf16[16,2,1500]{2,1,0:T(2,128)(2,1)}, u32[]{:S(2)}) copy-start(bf16[16,2,1500]{2,1,0:T(2,128)(2,1)} %param.5) | copy-start | bytes 288004
  17.3 2.6 %copy-start.8 = (s32[128]{0:T(128)S(1)}, s32[128]{0:T(128)}, u32[]{:S(2)}) copy-start(s32[128]{0:T(128)} %param.6) | copy-start | bytes 1540
  17.3 2.7 %copy-start.9 = (s32[8]{0:T(128)S(1)}, s32[8]{0:T(128)}, u32[]{:S(2)}) copy-start(s32[8]{0:T(128)} %param.7) | copy-start | bytes 100
  55.9 22.1 %all-to-all-start = ((bf16[128,2,1280]{2,1,0:T(2,128)(2,1)}), bf16[128,2,1280]{2,1,0:T(2,128)(2,1)S(1)}, u32[]{:S(2)}, u32[]{:S(2)}) async-start(bf16[128,2,1280]{2,1,0:T(2,128)(2,1)} %copy.28), calls=%async_computation | async-start | bytes 1310720 | tf_op jit(solution)/shard_map/all_to_all | solution.py:83
  82.9 0.8 copy-start.3
  86.8 1.7 %copy-start = (bf16[32,8,1280]{0,1,2:T(8,128)(2,1)S(1)}, bf16[32,8,1280]{0,1,2:T(8,128)(2,1)}, u32[]{:S(2)}) copy-start(bf16[32,8,1280]{0,1,2:T(8,128)(2,1)} %get-tuple-element.110) | copy-start | bytes 1966084 | tf_op jit(solution)/shard_map/while
  95.5 1.7 %copy-start.1 = (bf16[32,8,1280]{0,1,2:T(8,128)(2,1)S(1)}, bf16[32,8,1280]{0,1,2:T(8,128)(2,1)}, u32[]{:S(2)}) copy-start(bf16[32,8,1280]{0,1,2:T(8,128)(2,1)} %get-tuple-element.110) | copy-start | bytes 1966084 | tf_op jit(solution)/shard_map/while
  99.7 2.5 %copy-start.2 = (f32[8,32,640]{2,1,0:T(8,128)S(1)}, f32[8,32,640]{2,1,0:T(8,128)}, u32[]{:S(2)}) copy-start(f32[8,32,640]{2,1,0:T(8,128)} %copy.52) | copy-start | bytes 1966084 | tf_op jit(solution)/shard_map/while
  102.2 3.0 %copy-start.6 = (bf16[2,8,32,801]{3,2,1,0:T(8,128)(2,1)S(1)}, bf16[2,8,32,801]{3,2,1,0:T(8,128)(2,1)}, u32[]{:S(2)}) copy-start(bf16[2,8,32,801]{3,2,1,0:T(8,128)(2,1)} %get-tuple-element.102) | copy-start | bytes 2460676 | tf_op jit(solution)/shard_map/while
  102.2 4.0 %copy-start.4 = (bf16[2,8,8,1280]{3,1,0,2:T(8,128)(2,1)S(1)}, bf16[2,8,8,1280]{3,1,0,2:T(8,128)(2,1)}, u32[]{:S(2)}) copy-start(bf16[2,8,8,1280]{3,1,0,2:T(8,128)(2,1)} %copy-done.3) | copy-start | bytes 983044 | tf_op jit(solution)/shard_map/while
  105.2 0.9 copy-start.7
  106.2 0.8 copy-start.3
  110.1 1.7 %copy-start = (bf16[32,8,1280]{0,1,2:T(8,128)(2,1)S(1)}, bf16[32,8,1280]{0,1,2:T(8,128)(2,1)}, u32[]{:S(2)}) copy-start(bf16[32,8,1280]{0,1,2:T(8,128)(2,1)} %get-tuple-element.110) | copy-start | bytes 1966084 | tf_op jit(solution)/shard_map/while
  118.7 1.7 %copy-start.1 = (bf16[32,8,1280]{0,1,2:T(8,128)(2,1)S(1)}, bf16[32,8,1280]{0,1,2:T(8,128)(2,1)}, u32[]{:S(2)}) copy-start(bf16[32,8,1280]{0,1,2:T(8,128)(2,1)} %get-tuple-element.110) | copy-start | bytes 1966084 | tf_op jit(solution)/shard_map/while
  122.9 2.5 %copy-start.2 = (f32[8,32,640]{2,1,0:T(8,128)S(1)}, f32[8,32,640]{2,1,0:T(8,128)}, u32[]{:S(2)}) copy-start(f32[8,32,640]{2,1,0:T(8,128)} %copy.52) | copy-start | bytes 1966084 | tf_op jit(solution)/shard_map/while
  125.4 3.0 %copy-start.6 = (bf16[2,8,32,801]{3,2,1,0:T(8,128)(2,1)S(1)}, bf16[2,8,32,801]{3,2,1,0:T(8,128)(2,1)}, u32[]{:S(2)}) copy-start(bf16[2,8,32,801]{3,2,1,0:T(8,128)(2,1)} %get-tuple-element.102) | copy-start | bytes 2460676 | tf_op jit(solution)/shard_map/while
  125.4 4.0 %copy-start.4 = (bf16[2,8,8,1280]{3,1,0,2:T(8,128)(2,1)S(1)}, bf16[2,8,8,1280]{3,1,0,2:T(8,128)(2,1)}, u32[]{:S(2)}) copy-start(bf16[2,8,8,1280]{3,1,0,2:T(8,128)(2,1)} %copy-done.3) | copy-start | bytes 983044 | tf_op jit(solution)/shard_map/while
  128.5 0.9 copy-start.7
where the time goes:
time: 130 us; the launch traced here: 129 us
  blocking collectives  40.2 us (31%)
  local copies, waits for them, and re-layouts  35.4 us (27%)
  other arithmetic  29.5 us (23%)
  matrix products  20.4 us (16%)
  starting transfers between devices  3.48 us (3%)
    all_gather x1, blocking collectives, body(): every_channel = lax.all_gather(local, 'row', axis=0, tiled=True)  33.5 us
    another operation x2, other arithmetic  27.4 us
    while x28, local copies, waits for them, and re-layouts  7.03 us
    all_gather x1, blocking collectives, body(): row_spectra = lax.all_gather(local, 'col', axis=1, tiled=True)  6.76 us
    add x2, local copies, waits for them, and re-layouts, correlate(): jnp.einsum('imf,jmf->ijf', row_real, col_real, preferred_element_type=jnp...  6.06 us
    dot_general x2, matrix products, correlate(): jnp.dot(stacked.reshape(-1, 2 * nfreq), itab, preferred_element_type=jnp....  5.41 us
    sub x2, local copies, waits for them, and re-layouts, correlate(): jnp.einsum('imf,jmf->ijf', row_imag, col_real, preferred_element_type=jnp...  4.94 us
    all_to_all x1, local copies, waits for them, and re-layouts, body(): lax.all_to_all(every_channel, 'col', split_axis=0, concat_axis=1, tiled=T...  4.91 us
  transfers between devices with their start and end apart: 1, of which 0 were waited for; matrix products, arithmetic and copies ran while one was open for 9% of the time, Pallas kernels for 0%

commit v1 on v0

--- a/solution.py
+++ b/solution.py
@@ -78,7 +78,19 @@
     table = forward_table(length, F)
     own_valid = lax.dynamic_slice_in_dim(minute_valid, col_index * per_device, per_device)
     local = whiten(records, row_live, own_valid, table, BAND)
-    row_spectra = lax.all_gather(local, "col", axis=1, tiled=True)
+    work_now = jax.lax.axis_size("col")
+    arr_now = jax.lax.axis_index("col")
+    back, block_next, next_value = (work_now, arr_now, local.shape[1])
+    line_up = tuple(((s, (s + 1) % back) for s in range(back)))
+    row_spectra = jnp.zeros((*local.shape[:1], back * next_value, *local.shape[2:]), local.dtype)
+    v_now = local
+    for u in range(back):
+        w_next = (block_next - u) % back
+        row_spectra = lax.dynamic_update_slice_in_dim(
+            row_spectra, v_now, w_next * next_value, axis=1
+        )
+        if u < back - 1:
+            v_now = jax.lax.ppermute(v_now, axis_name="col", perm=line_up)
     every_channel = lax.all_gather(local, "row", axis=0, tiled=True)
     col_spectra = lax.all_to_all(every_channel, "col", split_axis=0, concat_axis=1, tiled=True)
     itab = inverse_table(length, F, MAXLAG)

time: 130 us -> 131 us (level)
  blocking collectives: 40.2 us -> 33 us
  waiting for transfers between devices: 0.01 us -> 7.07 us
    ppermute x0 -> x3, waiting for transfers between devices: none -> 7.06 us  [body(): v_now = jax.lax.ppermute(v_now, axis_name='col', perm=line_up)]
    all_gather x1 -> x0, blocking collectives: 6.76 us -> none  [body(): row_spectra = lax.all_gather(local, 'col', axis=1, tiled=True)]
  transfers between devices with their start and end apart: 1 -> 4, of which waited for: 0 -> 2; matrix products, arithmetic and copies ran while one was open for 9% -> 11% of each run, Pallas kernels for 0% -> 0%
where the time goes in v1:
time: 131 us
  local copies, waits for them, and re-layouts  35.9 us (27%)
  blocking collectives  33 us (25%)
  other arithmetic  29.5 us (23%)
  matrix products  20.4 us (16%)
  waiting for transfers between devices  7.07 us (5%)
  starting transfers between devices  4.53 us (3%)
    all_gather x1, blocking collectives, body(): every_channel = lax.all_gather(local, 'row', axis=0, tiled=True)  33 us
    another operation x2, other arithmetic  27.4 us
    ppermute x3, waiting for transfers between devices, body(): v_now = jax.lax.ppermute(v_now, axis_name='col', perm=line_up)  7.06 us
    while x28, local copies, waits for them, and re-layouts  7.02 us
    add x2, local copies, waits for them, and re-layouts, correlate(): jnp.einsum('imf,jmf->ijf', row_real, col_real, preferred_element_type=jnp...  6.13 us
    dot_general x2, matrix products, correlate(): jnp.dot(stacked.reshape(-1, 2 * nfreq), itab, preferred_element_type=jnp....  5.41 us
    all_to_all x1, local copies, waits for them, and re-layouts, body(): lax.all_to_all(every_channel, 'col', split_axis=0, concat_axis=1, tiled=T...  4.96 us
    sub x2, local copies, waits for them, and re-layouts, correlate(): jnp.einsum('imf,jmf->ijf', row_imag, col_real, preferred_element_type=jnp...  4.94 us
  transfers between devices with their start and end apart: 4, of which 2 were waited for; matrix products, arithmetic and copies ran while one was open for 11% of the time, Pallas kernels for 0%

profile of v1, /device:TPU:0, one launch (start us, length us, event | category | flops | bytes accessed | tf_op | source)
XLA Modules:
  0.0 130.8 jit_solution(11740698691924445887)
XLA Ops:
  0.0 17.2 %cosine_convert_fusion = (bf16[1500,640]{1,0:T(8,128)(2,1)S(1)}, bf16[1500,640]{1,0:T(8,128)(2,1)}) fusion(s32[640]{0:T(1024)S(1)} %iota_add_fusion.1), kind=kLoop, calls=%fused_computation.31 | loop fusion | flops 11520000 | bytes 3842560 | tf_op jit(solution)/shard_map/convert.2
  17.3 2.3 %fusion.45 = (f32[32,1280]{1,0:T(8,128)S(1)}, f32[32,1280]{1,0:T(8,128)S(1)}) fusion(bf16[32,1500]{1,0:T(8,128)(2,1)S(1)} %reshape.42, bf16[1500,640]{1,0:T(8,128)(2,1)} %get-tuple-element.61, bf16[1500,640]{1,0:T(8,128)(2,1)S(1)} %get-tuple-element.60), kind=kOutput, calls=%fused_computation.63 | convolution fusion | flops 130600960 | bytes 4263680 | tf_op jit(solution)/shard_map/dot_general | solution.py:31
  21.5 33.0 %all_gather.3 = bf16[128,2,1280]{2,0,1:T(8,128)(2,1)S(1)} all-gather(bf16[16,2,1280]{2,0,1:T(8,128)(2,1)S(1)} %fusion.39), channel_id=1, replica_groups=mesh['row'=8,'col'=4] {'row'}, dimensions={0}, use_global_device_ids=true | all-gather | bytes 737280 | tf_op jit(solution)/shard_map/all_gather | solution.py:94
  54.5 1.5 %copy.37 = bf16[128,2,1280]{2,1,0:T(2,128)(2,1)} copy(bf16[128,2,1280]{2,0,1:T(8,128)(2,1)S(1)} %all_gather.3) | data formatting | bytes 1310720 | tf_op jit(solution)/shard_map/all_gather | solution.py:94
  56.0 3.5 %all-to-all-start = ((bf16[128,2,1280]{2,1,0:T(2,128)(2,1)}), bf16[128,2,1280]{2,1,0:T(2,128)(2,1)S(1)}, u32[]{:S(2)}, u32[]{:S(2)}) async-start(bf16[128,2,1280]{2,1,0:T(2,128)(2,1)} %copy.37), calls=%async_computation | async-start | bytes 1310720 | tf_op jit(solution)/shard_map/all_to_all | solution.py:95
  59.5 10.2 %cosine_convert_fusion.1 = (bf16[640,801]{1,0:T(8,128)(2,1)S(1)}, bf16[640,801]{1,0:T(8,128)(2,1)S(1)}) fusion(s32[801]{0:T(1024)S(1)} %iota_add_fusion, s32[640]{0:T(1024)S(1)} %iota_add_fusion.1), kind=kLoop, calls=%fused_computation.41 | loop fusion | flops 6151680 | bytes 2056324 | tf_op jit(solution)/shard_map/convert
  69.9 1.6 %pad_maximum_fusion = bf16[1280,801]{1,0:T(8,128)(2,1)} fusion(bf16[640,801]{1,0:T(8,128)(2,1)S(1)} %get-tuple-element.59, bf16[640,801]{1,0:T(8,128)(2,1)S(1)} %get-tuple-element.58), kind=kLoop, calls=%fused_computation.39 | loop fusion | flops 4101120 | bytes 4101120 | tf_op jit(solution)/shard_map/concatenate | solution.py:25
  72.1 3.3 %collective-permute-done.1 = bf16[16,2,1280]{2,0,1:T(8,128)(2,1)S(1)} collective-permute-done((bf16[16,2,1280]{2,0,1:T(8,128)(2,1)S(1)}, bf16[16,2,1280]{2,0,1:T(8,128)(2,1)S(1)}, u32[]{:S(2)}, u32[]{:S(2)}) %collective-permute-start.1) | collective-permute-done | bytes 81952 | tf_op jit(solution)/shard_map/ppermute | solution.py:93
  75.5 3.7 %collective-permute-done.2 = bf16[16,2,1280]{2,0,1:T(8,128)(2,1)S(1)} collective-permute-done((bf16[16,2,1280]{2,0,1:T(8,128)(2,1)S(1)}, bf16[16,2,1280]{2,0,1:T(8,128)(2,1)S(1)}, u32[]{:S(2)}, u32[]{:S(2)}) %collective-permute-start.2) | collective-permute-done | bytes 81952 | tf_op jit(solution)/shard_map/ppermute | solution.py:93
  79.4 5.0 %copy.38 = bf16[32,4,2,1280]{0,2,1,3:T(2,128)(2,1)} copy(bf16[32,4,2,1280]{3,2,0,1:T(2,128)(2,1)S(1)} %bitcast.75) | data formatting | bytes 1310720 | tf_op jit(solution)/shard_map/all_to_all | solution.py:95
  84.3 46.5 %while.10 = (s32[]{:T(128)}, bf16[2,8,32,801]{3,2,1,0:T(8,128)(2,1)}, bf16[2,8,8,1280]{3,2,1,0:T(8,128)(2,1)S(1)}, bf16[32,8,1280]{0,1,2:T(8,128)(2,1)}, bf16[1280,801]{1,0:T(8,128)(2,1)}, /*index=5*/s32[]{:T(128)}) while((s32[]{:T(128)}, bf16[2,8,32,801]{3,2,1,0:T(8,128)(2,1)}, bf16[2,8,8,1280]{3,2,1,0:T(8,128)(2,1)S(1)}, ...), condition=%wide.region_2.3_spmd, body=%wide.region_1.2_spmd.sunk | while | flops 537149952 | bytes 34353424 | solution.py:103
  85.1 1.7 %copy.61 = bf16[1,8,8,1280]{2,1,3,0:T(8,128)(2,1)S(1)} copy(bf16[1,8,8,1280]{3,2,1,0:T(8,128)(2,1)S(1)} %constant_dynamic-slice_fusion.2) | data formatting | bytes 327680 | tf_op jit(solution)/shard_map/while/body/jit(dynamic_index_in_dim)/dynamic_slice | solution.py:103
  86.8 1.4 %fusion.98 = bf16[32,8,640]{0,1,2:T(8,128)(2,1)S(1)} fusion(bf16[32,8,1280]{0,1,2:T(8,128)(2,1)} %get-tuple-element.110), kind=kLoop, calls=%fused_computation.15.clone.1.clone.1 | loop fusion | bytes 655360 | tf_op jit(solution)/shard_map/while/body/eval_jaxpr/imf,jmf->ijf/dot_general | solution.py:54
  89.1 0.9 copy-done
  90.1 2.4 %add_bitcast_fusion.2 = f32[8,32,640]{1,0,2:T(8,128)} fusion(f32[640,8,32]{2,1,0:T(8,128)S(1)} %fusion.99, bf16[1,8,8,1280]{2,1,3,0:T(8,128)(2,1)S(1)} %copy.61, bf16[32,8,640]{0,1,2:T(8,128)(2,1)S(1)} %fusion.100), kind=kOutput, calls=%fused_computation.9.clone.2 | convolution fusion | flops 2785280 | bytes 1802240 | tf_op jit(solution)/shard_map/while/body/eval_jaxpr/imf,jmf->ijf/dot_general | solution.py:52
  92.4 3.1 %copy.63 = f32[8,32,640]{2,1,0:T(8,128)} copy(f32[8,32,640]{1,0,2:T(8,128)} %add_bitcast_fusion.2) | data formatting | bytes 1310720 | tf_op jit(solution)/shard_map/while/body/eval_jaxpr/add | solution.py:52
  95.5 1.4 %fusion.95 = bf16[32,8,640]{0,1,2:T(8,128)(2,1)S(1)} fusion(bf16[32,8,1280]{0,1,2:T(8,128)(2,1)} %get-tuple-element.110), kind=kLoop, calls=%fused_computation.16.clone.1.clone.1 | loop fusion | bytes 655360 | tf_op jit(solution)/shard_map/while/body/eval_jaxpr/imf,jmf->ijf/dot_general | solution.py:55
  97.7 0.9 copy-done.1
  98.7 2.4 %subtract_bitcast_fusion.2 = f32[8,32,640]{1,0,2:T(8,128)} fusion(f32[640,8,32]{2,1,0:T(8,128)S(1)} %fusion.96, bf16[1,8,8,1280]{2,1,3,0:T(8,128)(2,1)S(1)} %copy.61, bf16[32,8,640]{0,1,2:T(8,128)(2,1)S(1)} %fusion.97), kind=kOutput, calls=%fused_computation.8.clone.2 | convolution fusion | flops 2785280 | bytes 1802240 | tf_op jit(solution)/shard_map/while/body/eval_jaxpr/imf,jmf->ijf/dot_general | solution.py:57
  101.1 2.5 %copy.62 = f32[8,32,640]{2,1,0:T(8,128)S(1)} copy(f32[8,32,640]{1,0,2:T(8,128)} %subtract_bitcast_fusion.2) | data formatting | bytes 1310720 | tf_op jit(solution)/shard_map/while/body/eval_jaxpr/sub | solution.py:55
  103.6 2.7 %fusion.101 = bf16[256,801]{0,1:T(8,128)(2,1)S(1)} fusion(bf16[1280,801]{1,0:T(8,128)(2,1)} %get-tuple-element.111, f32[256,640]{1,0:T(8,128)S(1)} %bitcast.73, f32[256,640]{1,0:T(8,128)S(1)} %bitcast.72), kind=kOutput, calls=%fused_computation.13.clone.1 | convolution fusion | flops 526336512 | bytes 3771392 | tf_op jit(solution)/shard_map/while/body/eval_jaxpr/dot_general | solution.py:61
  106.7 0.9 copy-done.7
  108.4 1.7 %copy.61 = bf16[1,8,8,1280]{2,1,3,0:T(8,128)(2,1)S(1)} copy(bf16[1,8,8,1280]{3,2,1,0:T(8,128)(2,1)S(1)} %constant_dynamic-slice_fusion.2) | data formatting | bytes 327680 | tf_op jit(solution)/shard_map/while/body/jit(dynamic_index_in_dim)/dynamic_slice | solution.py:103
  110.1 1.4 %fusion.98 = bf16[32,8,640]{0,1,2:T(8,128)(2,1)S(1)} fusion(bf16[32,8,1280]{0,1,2:T(8,128)(2,1)} %get-tuple-element.110), kind=kLoop, calls=%fused_computation.15.clone.1.clone.1 | loop fusion | bytes 655360 | tf_op jit(solution)/shard_map/while/body/eval_jaxpr/imf,jmf->ijf/dot_general | solution.py:54
  112.3 0.9 copy-done
  113.3 2.4 %add_bitcast_fusion.2 = f32[8,32,640]{1,0,2:T(8,128)} fusion(f32[640,8,32]{2,1,0:T(8,128)S(1)} %fusion.99, bf16[1,8,8,1280]{2,1,3,0:T(8,128)(2,1)S(1)} %copy.61, bf16[32,8,640]{0,1,2:T(8,128)(2,1)S(1)} %fusion.100), kind=kOutput, calls=%fused_computation.9.clone.2 | convolution fusion | flops 2785280 | bytes 1802240 | tf_op jit(solution)/shard_map/while/body/eval_jaxpr/imf,jmf->ijf/dot_general | solution.py:52
  115.7 3.1 %copy.63 = f32[8,32,640]{2,1,0:T(8,128)} copy(f32[8,32,640]{1,0,2:T(8,128)} %add_bitcast_fusion.2) | data formatting | bytes 1310720 | tf_op jit(solution)/shard_map/while/body/eval_jaxpr/add | solution.py:52
  118.7 1.4 %fusion.95 = bf16[32,8,640]{0,1,2:T(8,128)(2,1)S(1)} fusion(bf16[32,8,1280]{0,1,2:T(8,128)(2,1)} %get-tuple-element.110), kind=kLoop, calls=%fused_computation.16.clone.1.clone.1 | loop fusion | bytes 655360 | tf_op jit(solution)/shard_map/while/body/eval_jaxpr/imf,jmf->ijf/dot_general | solution.py:55
  121.0 0.9 copy-done.1
  122.0 2.4 %subtract_bitcast_fusion.2 = f32[8,32,640]{1,0,2:T(8,128)} fusion(f32[640,8,32]{2,1,0:T(8,128)S(1)} %fusion.96, bf16[1,8,8,1280]{2,1,3,0:T(8,128)(2,1)S(1)} %copy.61, bf16[32,8,640]{0,1,2:T(8,128)(2,1)S(1)} %fusion.97), kind=kOutput, calls=%fused_computation.8.clone.2 | convolution fusion | flops 2785280 | bytes 1802240 | tf_op jit(solution)/shard_map/while/body/eval_jaxpr/imf,jmf->ijf/dot_general | solution.py:57
  124.4 2.5 %copy.62 = f32[8,32,640]{2,1,0:T(8,128)S(1)} copy(f32[8,32,640]{1,0,2:T(8,128)} %subtract_bitcast_fusion.2) | data formatting | bytes 1310720 | tf_op jit(solution)/shard_map/while/body/eval_jaxpr/sub | solution.py:55
  126.9 2.7 %fusion.101 = bf16[256,801]{0,1:T(8,128)(2,1)S(1)} fusion(bf16[1280,801]{1,0:T(8,128)(2,1)} %get-tuple-element.111, f32[256,640]{1,0:T(8,128)S(1)} %bitcast.73, f32[256,640]{1,0:T(8,128)S(1)} %bitcast.72), kind=kOutput, calls=%fused_computation.13.clone.1 | convolution fusion | flops 526336512 | bytes 3771392 | tf_op jit(solution)/shard_map/while/body/eval_jaxpr/dot_general | solution.py:61
  (66 shorter events, 9.6 us)
Async XLA Ops:
  0.0 17.2 %copy-start.5 = (bf16[16,2,1500]{2,1,0:T(2,128)(2,1)S(1)}, bf16[16,2,1500]{2,1,0:T(2,128)(2,1)}, u32[]{:S(2)}) copy-start(bf16[16,2,1500]{2,1,0:T(2,128)(2,1)} %param.5) | copy-start | bytes 288004
  17.3 2.6 %copy-start.8 = (s32[8]{0:T(128)S(1)}, s32[8]{0:T(128)}, u32[]{:S(2)}) copy-start(s32[8]{0:T(128)} %param.7) | copy-start | bytes 100
  17.3 2.7 %copy-start.9 = (s32[128]{0:T(128)S(1)}, s32[128]{0:T(128)}, u32[]{:S(2)}) copy-start(s32[128]{0:T(128)} %param.6) | copy-start | bytes 1540
  20.9 50.6 %collective-permute-start = (bf16[16,2,1280]{2,0,1:T(8,128)(2,1)S(1)}, bf16[16,2,1280]{2,0,1:T(8,128)(2,1)S(1)}, u32[]{:S(2)}, u32[]{:S(2)}) collective-permute-start(bf16[16,2,1280]{2,0,1:T(8,128)(2,1)S(1)} %fusion.39), channel_id=1, source_target_pairs={{0,1},{1,2},{2,3},{3,0},{4,5},{5,6},{6,7},{7,4},{8,9},{9,10},{10,1... | collective-permute-start | bytes 245768 | tf_op jit(solution)/shard_map/ppermute | solution.py:93
  56.0 23.3 %all-to-all-start = ((bf16[128,2,1280]{2,1,0:T(2,128)(2,1)}), bf16[128,2,1280]{2,1,0:T(2,128)(2,1)S(1)}, u32[]{:S(2)}, u32[]{:S(2)}) async-start(bf16[128,2,1280]{2,1,0:T(2,128)(2,1)} %copy.37), calls=%async_computation | async-start | bytes 1310720 | tf_op jit(solution)/shard_map/all_to_all | solution.py:95
  71.5 3.9 %collective-permute-start.1 = (bf16[16,2,1280]{2,0,1:T(8,128)(2,1)S(1)}, bf16[16,2,1280]{2,0,1:T(8,128)(2,1)S(1)}, u32[]{:S(2)}, u32[]{:S(2)}) collective-permute-start(bf16[16,2,1280]{2,0,1:T(8,128)(2,1)S(1)} %collective-permute-done), channel_id=1, source_target_pairs={{0,1},{1,2},{2,3},{3,0},{4,5},{5,6},{6,7},{7,4},{8,9},{9,10},{10,1... | collective-permute-start | bytes 245768 | tf_op jit(solution)/shard_map/ppermute | solution.py:93
  75.4 3.9 %collective-permute-start.2 = (bf16[16,2,1280]{2,0,1:T(8,128)(2,1)S(1)}, bf16[16,2,1280]{2,0,1:T(8,128)(2,1)S(1)}, u32[]{:S(2)}, u32[]{:S(2)}) collective-permute-start(bf16[16,2,1280]{2,0,1:T(8,128)(2,1)S(1)} %collective-permute-done.1), channel_id=1, source_target_pairs={{0,1},{1,2},{2,3},{3,0},{4,5},{5,6},{6,7},{7,4},{8,9},{9,10},{10,1... | collective-permute-start | bytes 245768 | tf_op jit(solution)/shard_map/ppermute | solution.py:93
  84.3 0.8 copy-start.3
  88.2 1.7 %copy-start = (bf16[32,8,1280]{0,1,2:T(8,128)(2,1)S(1)}, bf16[32,8,1280]{0,1,2:T(8,128)(2,1)}, u32[]{:S(2)}) copy-start(bf16[32,8,1280]{0,1,2:T(8,128)(2,1)} %get-tuple-element.110) | copy-start | bytes 1966084 | tf_op jit(solution)/shard_map/while
  96.9 1.7 %copy-start.1 = (bf16[32,8,1280]{0,1,2:T(8,128)(2,1)S(1)}, bf16[32,8,1280]{0,1,2:T(8,128)(2,1)}, u32[]{:S(2)}) copy-start(bf16[32,8,1280]{0,1,2:T(8,128)(2,1)} %get-tuple-element.110) | copy-start | bytes 1966084 | tf_op jit(solution)/shard_map/while
  101.1 2.5 %copy-start.2 = (f32[8,32,640]{2,1,0:T(8,128)S(1)}, f32[8,32,640]{2,1,0:T(8,128)}, u32[]{:S(2)}) copy-start(f32[8,32,640]{2,1,0:T(8,128)} %copy.63) | copy-start | bytes 1966084 | tf_op jit(solution)/shard_map/while
  103.6 3.0 %copy-start.6 = (bf16[2,8,32,801]{3,2,1,0:T(8,128)(2,1)S(1)}, bf16[2,8,32,801]{3,2,1,0:T(8,128)(2,1)}, u32[]{:S(2)}) copy-start(bf16[2,8,32,801]{3,2,1,0:T(8,128)(2,1)} %get-tuple-element.102) | copy-start | bytes 2460676 | tf_op jit(solution)/shard_map/while
  103.6 4.0 %copy-start.4 = (bf16[2,8,8,1280]{3,2,1,0:T(8,128)(2,1)S(1)}, bf16[2,8,8,1280]{3,2,1,0:T(8,128)(2,1)}, u32[]{:S(2)}) copy-start(bf16[2,8,8,1280]{3,2,1,0:T(8,128)(2,1)} %copy-done.3) | copy-start | bytes 983044 | tf_op jit(solution)/shard_map/while
  106.7 0.9 copy-start.7
  107.6 0.8 copy-start.3
  111.5 1.7 %copy-start = (bf16[32,8,1280]{0,1,2:T(8,128)(2,1)S(1)}, bf16[32,8,1280]{0,1,2:T(8,128)(2,1)}, u32[]{:S(2)}) copy-start(bf16[32,8,1280]{0,1,2:T(8,128)(2,1)} %get-tuple-element.110) | copy-start | bytes 1966084 | tf_op jit(solution)/shard_map/while
  120.1 1.7 %copy-start.1 = (bf16[32,8,1280]{0,1,2:T(8,128)(2,1)S(1)}, bf16[32,8,1280]{0,1,2:T(8,128)(2,1)}, u32[]{:S(2)}) copy-start(bf16[32,8,1280]{0,1,2:T(8,128)(2,1)} %get-tuple-element.110) | copy-start | bytes 1966084 | tf_op jit(solution)/shard_map/while
  124.4 2.5 %copy-start.2 = (f32[8,32,640]{2,1,0:T(8,128)S(1)}, f32[8,32,640]{2,1,0:T(8,128)}, u32[]{:S(2)}) copy-start(f32[8,32,640]{2,1,0:T(8,128)} %copy.63) | copy-start | bytes 1966084 | tf_op jit(solution)/shard_map/while
  126.8 3.0 %copy-start.6 = (bf16[2,8,32,801]{3,2,1,0:T(8,128)(2,1)S(1)}, bf16[2,8,32,801]{3,2,1,0:T(8,128)(2,1)}, u32[]{:S(2)}) copy-start(bf16[2,8,32,801]{3,2,1,0:T(8,128)(2,1)} %get-tuple-element.102) | copy-start | bytes 2460676 | tf_op jit(solution)/shard_map/while
  126.9 4.0 %copy-start.4 = (bf16[2,8,8,1280]{3,2,1,0:T(8,128)(2,1)S(1)}, bf16[2,8,8,1280]{3,2,1,0:T(8,128)(2,1)}, u32[]{:S(2)}) copy-start(bf16[2,8,8,1280]{3,2,1,0:T(8,128)(2,1)} %copy-done.3) | copy-start | bytes 983044 | tf_op jit(solution)/shard_map/while
  129.9 0.9 copy-start.7
